TPU v7x, 32 devices: a whole 2x2x4 slice. The times are simulated.
32 devices in a mesh: img: 8 (over z, core), row: 4 (over y, x).
Axes of the slice: x: 2, y: 2, z: 4, core: 2. Of those that a mesh axis runs over, the one named last changes fastest.
Arguments:
- features: float32 [32, 1024, 256], P('img', 'row'), may hold values from -8 to 8
- partners: int32 [32, 2], replicated, may hold values from 0 to 31, as said below
- counts: int32 [32], replicated, may hold values from 256 to 1024, as said below
- shared_proj: bfloat16 [256, 256], replicated, may hold values from -0.375 to 0.375
- value_proj: bfloat16 [256, 256], replicated, may hold values from -0.375 to 0.375
- out_proj: bfloat16 [256, 256], replicated, may hold values from -0.375 to 0.375
- ffn_in: bfloat16 [512, 512], replicated, may hold values from -0.25 to 0.25
- ffn_in_bias: float32 [512], replicated, may hold values from -3 to 3
- norm_gain: float32 [512], replicated, may hold values from 0.1 to 1.9
- norm_bias: float32 [512], replicated, may hold values from -3 to 3
- ffn_out: bfloat16 [512, 256], replicated, may hold values from -0.25 to 0.25
- ffn_out_bias: float32 [256], replicated, may hold values from -3 to 3
Outputs:
- refined: float32 [32, 1024, 256], P('img', 'row')
Inputs may be any that keep to these rules, and one draw needn't show every extreme that they name: Images form blocks of 4 consecutive ones around a cycle of blocks. Both partners of an image lie in a block at distance 1 or 2 from its own block in either direction around the cycle. Of the 8 partner entries of one block, at most 3 lie in any one of those four blocks, and in every block exactly 3 lie in one of them. Keypoint slots at positions counts[i] and beyond of image i are padding; counts may equal 1024.
All inputs are finite; a program needn't handle non-finite values.
Results may differ from a plain program's by a relative error of at most 0.004.
Values may be sent and summed in bfloat16 or wider, within the bound.
No kernel may reach another device: no remote copies, remote signals or barrier semaphores. Data moves between devices by JAX's collectives and lax.ppermute only.
A program may use at most 64 MiB of HBM per device.

v0:
```python
import functools
import math

import jax
import jax.numpy as jnp
from jax import lax
from jax.experimental import pallas as pl
from jax.experimental.pallas import tpu as pltpu
from jax.sharding import PartitionSpec as P

HEADS = 4
LEAST, MOST = 1e-25, 1e25
NEGATIVE = -1e30
VMEM = 60 * 2**20
NT = (((1,), (1,)), ((), ()))
F32 = jnp.float32
BF16 = jnp.bfloat16

COMPANION, THICK, THIN, CROSS = range(4)


def block_of(kind, me, img_count):
    odd = lax.rem(me, 2)
    ahead = 1 - 2 * odd
    step = {COMPANION: ahead, THICK: 2 * ahead, THIN: -2 * ahead, CROSS: -ahead}[kind]
    return lax.rem(me + step + img_count, img_count)


def whole(memory=pltpu.VMEM):
    return pl.BlockSpec(memory_space=memory)


def exchange(value):
    return lax.all_to_all(value, "row", split_axis=0, concat_axis=0, tiled=True)


def project_kernel(head_dim, rows, shared_proj, value_proj, out):
    heads, _, lanes = out.shape
    low = lax.broadcasted_iota(jnp.int32, (1, lanes), 1) < head_dim
    for pair in range(heads // 2):
        columns = slice(pair * lanes, (pair + 1) * lanes)
        turned = pltpu.roll(value_proj[:, columns].astype(F32), head_dim, 1).astype(BF16)
        both = jnp.concatenate([shared_proj[:, columns], turned], axis=1)
        projected = jnp.dot(rows[...], both, preferred_element_type=F32)
        shared, values = projected[:, :lanes], projected[:, lanes:]
        out[2 * pair] = jnp.where(low, shared, values).astype(BF16)
        out[2 * pair + 1] = jnp.where(low, values, shared).astype(BF16)


def project(value, shared_proj, value_proj, row_devices, after=(), weigh=1):
    per_dev, row_count, width = value.shape
    rows = per_dev * row_count
    head_dim = width // HEADS

    def kernel(rows_ref, shared_ref, value_ref, *refs):
        project_kernel(head_dim, rows_ref, shared_ref, value_ref, refs[-1])

    packed = pl.pallas_call(
        kernel,
        out_shape=jax.ShapeDtypeStruct((HEADS, rows, 2 * head_dim), BF16),
        in_specs=[whole()] * 3 + [whole(pl.ANY)] * len(after),
        out_specs=whole(),
        compiler_params=pltpu.CompilerParams(vmem_limit_bytes=VMEM),
        cost_estimate=pl.CostEstimate(
            flops=weigh * 4 * rows * width * width, bytes_accessed=6 * rows * width, transcendentals=0
        ),
        name="project",
    )(value.reshape(rows, width), shared_proj, value_proj, *after)
    if row_devices > HEADS:
        packed = jnp.repeat(packed, row_devices // HEADS, axis=0)
    return exchange(packed)


def tie(value, after):
    def kernel(value_ref, after_ref, out_ref):
        pass

    return pl.pallas_call(
        kernel,
        out_shape=jax.ShapeDtypeStruct(value.shape, value.dtype),
        in_specs=[whole(pltpu.HBM)] * 2,
        out_specs=whole(pltpu.HBM),
        input_output_aliases={0: 0},
        name="tie",
    )(value, after)


def attend_kernel(kinds, first, last, head_dim, counts, partners, own_hbm, *refs):
    blocks_hbm, refs = refs[:len(kinds)], refs[len(kinds):]
    if first:
        out_hbm, own, blocks, total, limits, todo, arrived, out, left = refs
    else:
        carried_hbm, out_hbm, own, blocks, total, limits, todo, arrived, out, left, carried, carried_here = refs
    devices, flat_rows, lanes = own.shape
    img_count = lax.axis_size("img")
    me = lax.axis_index("img")
    per_dev = counts.shape[0] // img_count
    row_count = flat_rows // per_dev
    keypoints = devices * row_count
    once = max(256, row_count)
    sources = once // row_count
    factor = head_dim ** (-0.5) * math.log2(math.e)

    copies = []
    for number, (source, target) in enumerate(
        [(own_hbm, own)] + [(block, blocks.at[place]) for place, block in enumerate(blocks_hbm)]
    ):
        for device in range(devices):
            copies.append(
                pltpu.make_async_copy(source.at[device], target.at[device], arrived.at[number, device])
            )
    for copy in copies:
        copy.start()
    if not first:
        carry_copy = pltpu.make_async_copy(carried_hbm, carried, carried_here)
        carry_copy.start()

    key_side = lax.rem(lax.div(lax.axis_index("row"), devices // HEADS), 2)
    lane_side = lax.broadcasted_iota(jnp.int32, (1, lanes), 1) // head_dim
    key_row = lax.broadcasted_iota(jnp.int32, (keypoints, 1), 0)
    key_lane = lax.broadcasted_iota(jnp.int32, (1, keypoints), 1)
    one, zero = jnp.ones((), BF16), jnp.zeros((), BF16)
    total[...] = jnp.zeros_like(total)
    limits[...] = jnp.ones_like(limits)

    pairs = jnp.zeros((), jnp.int32)
    for place, kind in enumerate(kinds):
        block_id = block_of(kind, me, img_count)
        for other in range(per_dev):
            for image in range(per_dev):
                theirs, mine = block_id * per_dev + other, me * per_dev + image
                times = jnp.zeros((), jnp.int32)
                for side in range(2):
                    times += (partners[2 * mine + side] == theirs).astype(jnp.int32)
                    times += (partners[2 * theirs + side] == mine).astype(jnp.int32)
                todo[0, pairs] = place * per_dev + other
                todo[1, pairs] = image
                todo[2, pairs] = times
                todo[3, pairs] = counts[theirs]
                pairs = pairs + (times > 0).astype(jnp.int32)
    for copy in copies:
        copy.wait()

    def image_rows(image):
        return pl.ds(pl.multiple_of(image * row_count, row_count), row_count)

    def operands(number):
        other, image, limit = todo[0, number], todo[1, number], todo[3, number]
        place, other = lax.div(other, per_dev), lax.rem(other, per_dev)
        tile = blocks[place, :, image_rows(other), :].reshape(keypoints, lanes)
        is_key, present = lane_side == key_side, key_row < limit
        keys = jnp.where(present, jnp.where(is_key, tile, zero), zero)
        values = jnp.where(present, jnp.where(is_key, one, tile), zero)
        return image, keys, values, limit, todo[2, number].astype(F32)

    def score(image, start, keys):
        queries = own[start:start + sources, image_rows(image), :].reshape(once, lanes)
        return lax.dot_general(queries, keys, NT, preferred_element_type=F32)

    def add(image, start, got, times):
        rows = slice(start * row_count, start * row_count + once)
        total[image, rows] += got * times / pltpu.roll(got, head_dim, 1)

    def fast(numbers):
        work = [operands(number) for number in numbers]
        least, most = limits[0], limits[1]
        for start in range(0, devices, sources):
            results = []
            for image, keys, values, _, times in work:
                raised = jnp.exp2(score(image, start, keys) * factor).astype(BF16)
                got = jnp.dot(raised, values, preferred_element_type=F32)
                by_row = got.reshape(once // 8, 8, lanes)
                least = jnp.minimum(least, jnp.min(by_row, axis=0))
                most = jnp.maximum(most, jnp.max(by_row, axis=0))
                results.append(got)
            for (image, _, _, _, times), got in zip(work, results):
                add(image, start, got, times)
        limits[0] = least
        limits[1] = most

    def slow(number, carry):
        image, keys, values, limit, times = operands(number)
        present = key_lane < limit
        for start in range(0, devices, sources):
            scores = score(image, start, keys)
            peak = jnp.max(jnp.where(present, scores, NEGATIVE), axis=1, keepdims=True)
            raised = jnp.where(present, jnp.exp2((scores - peak) * factor), 0.0).astype(BF16)
            add(image, start, jnp.dot(raised, values, preferred_element_type=F32), times)
        return carry

    def two(number, carry):
        fast((2 * number, 2 * number + 1))
        return carry

    lax.fori_loop(0, pairs // 2, two, 0)

    @pl.when(pairs % 2 == 1)
    def _():
        fast((pairs - 1,))

    outside = (limits[0] < LEAST) | (limits[1] > MOST)
    outside = jnp.where((lane_side == key_side) & outside, 1.0, 0.0)

    @pl.when(jnp.max(outside) > 0.5)
    def _():
        total[...] = jnp.zeros_like(total)
        lax.fori_loop(0, pairs, slow, 0)

    if not first:
        carry_copy.wait()
    gone = []
    for pair in range(per_dev // 2):
        even, uneven = total[2 * pair], total[2 * pair + 1]
        even_low = jnp.where(key_side == 1, even, pltpu.roll(even, head_dim, 1))
        uneven_high = jnp.where(key_side == 0, uneven, pltpu.roll(uneven, head_dim, 1))
        both = jnp.where(lane_side == 0, even_low, uneven_high)
        if not first:
            both += carried[pair]
        if last:
            place = (slice(None), slice(pair * row_count, (pair + 1) * row_count))
            out[place] = both.astype(BF16).reshape(devices, row_count, lanes)
        else:
            place = (pair,)
            out[pair] = both
        gone.append(pltpu.make_async_copy(out.at[place], out_hbm.at[place], left.at[pair]))
        gone[-1].start()
    for copy in gone:
        copy.wait()


def attend(kinds, last, head_dim, counts, partners, own, blocks, carried):
    devices, flat_rows, lanes = own.shape
    per_dev = counts.shape[0] // lax.axis_size("img")
    keypoints = devices * flat_rows // per_dev
    packed = (per_dev // 2, keypoints, lanes)
    first = carried is None
    arguments = [counts, partners, own, *blocks] + ([] if first else [carried])
    if last:
        out_shape = jax.ShapeDtypeStruct((devices, flat_rows // 2, lanes), BF16)
    else:
        out_shape = jax.ShapeDtypeStruct(packed, F32)
    scratch = [
        pltpu.VMEM(own.shape, BF16),
        pltpu.VMEM((len(kinds), *own.shape), BF16),
        pltpu.VMEM((per_dev, keypoints, lanes), F32),
        pltpu.VMEM((2, 8, lanes), F32),
        pltpu.SMEM((4, len(kinds) * per_dev * per_dev + 1), jnp.int32),
        pltpu.SemaphoreType.DMA((1 + len(kinds), devices)),
        pltpu.VMEM(out_shape.shape, out_shape.dtype),
        pltpu.SemaphoreType.DMA((per_dev // 2,)),
    ]
    if not first:
        scratch += [pltpu.VMEM(packed, F32), pltpu.SemaphoreType.DMA]
    return pl.pallas_call(
        functools.partial(attend_kernel, kinds, first, last, head_dim),
        out_shape=out_shape,
        in_specs=[whole(pltpu.SMEM)] * 2 + [whole(pltpu.HBM)] * (len(arguments) - 2),
        out_specs=whole(pltpu.HBM),
        scratch_shapes=scratch,
        compiler_params=pltpu.CompilerParams(vmem_limit_bytes=VMEM),
        cost_estimate=pl.CostEstimate(
            flops=0 if first else len(kinds) * 4 * 2 * 2 * keypoints * keypoints * 512,
            bytes_accessed=0 if first else 4 * devices * flat_rows * lanes + 8 * keypoints * lanes,
            transcendentals=0 if first else len(kinds) * 4 * keypoints * keypoints,
        ),
        name="attend_" + "_".join(str(kind) for kind in kinds),
    )(*arguments)


def refine_kernel(head_dim, everyone, features, messages, out_proj, ffn_in, ffn_in_bias, norm_gain,
                  norm_bias, ffn_out, ffn_out_bias, out):
    together, row_count, width = features.shape
    lanes = 2 * head_dim
    pair = pl.program_id(0)
    first_image = (lax.axis_index("img") * pl.num_programs(0) + pair) * together
    lane_side = lax.broadcasted_iota(jnp.int32, (1, lanes), 1) // head_dim
    tiles = [messages[head, 0].astype(F32) for head in range(HEADS)]
    turned = [pltpu.roll(tile, head_dim, 1) for tile in tiles]
    averaged = []
    for image in range(together):
        low, high = (tiles, turned) if image == 0 else (turned, tiles)
        inbox = jnp.concatenate(
            [jnp.where(lane_side == 0, low[head], high[head + 1]) for head in range(0, HEADS, 2)], axis=1
        )
        asked = (everyone[...] == first_image + image).astype(F32)
        degree = jnp.sum(asked, axis=1, keepdims=True)
        averaged.append((inbox / (2.0 + degree)).astype(BF16))
    averaged = jnp.concatenate(averaged, axis=0)
    projected = jnp.dot(averaged, out_proj[...], preferred_element_type=F32).astype(BF16)
    source = features[...].reshape(together * row_count, width)
    hidden = (
        jnp.dot(source.astype(BF16), ffn_in[:width], preferred_element_type=F32)
        + jnp.dot(projected, ffn_in[width:], preferred_element_type=F32)
        + ffn_in_bias[...]
    )
    hidden = hidden - jnp.mean(hidden, axis=1, keepdims=True)
    spread = jnp.mean(hidden * hidden, axis=1, keepdims=True)
    normed = hidden * lax.rsqrt(spread + 1e-05) * norm_gain[...] + norm_bias[...]
    activated = (0.5 * normed * (1.0 + lax.erf(normed * (0.5**0.5)))).astype(BF16)
    refined = source + jnp.dot(activated, ffn_out[...], preferred_element_type=F32) + ffn_out_bias[...]
    out[...] = refined.reshape(together, row_count, width)


def per_device(features, partners, counts, shared_proj, value_proj, out_proj, ffn_in, ffn_in_bias,
               norm_gain, norm_bias, ffn_out, ffn_out_bias):
    img_count = lax.axis_size("img")
    row_devices = lax.axis_size("row")
    per_dev, row_count, width = features.shape
    head_dim = width // HEADS
    blocks = range(img_count)
    swap = [(s, s ^ 1) for s in blocks]
    thick_pairs = [(s, (s + (2 if s % 2 else -2)) % img_count) for s in blocks]
    thin_pairs = [(s, (s + (-2 if s % 2 else 2)) % img_count) for s in blocks]

    rounded = features.astype(BF16)
    thick = lax.ppermute(rounded, "img", thick_pairs)
    thin = lax.ppermute(rounded, "img", thin_pairs)
    flat_partners = partners.reshape(-1)

    weights = (shared_proj, value_proj, row_devices)
    own = project(rounded, *weights)
    companion = lax.ppermute(own, "img", swap)
    thick = project(thick, *weights, weigh=50)
    work = functools.partial(attend, head_dim=head_dim, counts=counts, partners=flat_partners, own=own)
    sums = work((COMPANION,), False, blocks=[companion], carried=None)
    thick = tie(thick, sums)
    cross = lax.ppermute(thick, "img", swap)
    thin = project(thin, *weights, after=(sums,), weigh=50)
    sums = work((THICK, CROSS), False, blocks=[thick, cross], carried=sums)
    messages = work((THIN,), True, blocks=[thin], carried=sums)
    messages = exchange(messages)[::row_devices // HEADS].reshape(HEADS, per_dev // 2, row_count, 2 * head_dim)

    pair = pl.BlockSpec((2, row_count, width), lambda i: (i, 0, 0))
    return pl.pallas_call(
        functools.partial(refine_kernel, head_dim),
        grid=(per_dev // 2,),
        out_shape=jax.ShapeDtypeStruct(features.shape, F32),
        in_specs=[
            whole(), pair, pl.BlockSpec((HEADS, 1, row_count, 2 * head_dim), lambda i: (0, i, 0, 0)),
        ] + [whole()] * 7,
        out_specs=pair,
        compiler_params=pltpu.CompilerParams(vmem_limit_bytes=VMEM // 3),
        cost_estimate=pl.CostEstimate(
            flops=10 * per_dev * row_count * width * width * 2, bytes_accessed=2**22, transcendentals=2**20
        ),
        name="refine",
    )(flat_partners[None], features, messages, out_proj, ffn_in, ffn_in_bias[None], norm_gain[None],
      norm_bias[None], ffn_out, ffn_out_bias[None])


def solution(mesh):
    return jax.shard_map(
        per_device,
        mesh=mesh,
        in_specs=(P("img", "row", None), P(), P(), P(), P(), P(), P(), P(), P(), P(), P(), P()),
        out_specs=P("img", "row", None),
        check_vma=False,
    )
```

profile of v0, /device:TPU:16, one launch (start us, length us, event | category | flops | bytes accessed | tf_op | source)
XLA Modules:
  0.0 125.0 jit_solution(1545453361514807150)
XLA Ops:
  0.0 2.1 %convert_element_type.3 = bf16[4,256,256]{2,1,0:T(8,128)(2,1)} convert(f32[4,256,256]{2,1,0:T(8,128)} %features.1) | non-fusion elementwise | flops 262144 | bytes 1572864 | tf_op jit(solution)/shard_map/convert_element_type | solution.py:315
  2.1 2.6 %project.3 = bf16[4,1024,128]{2,1,0:T(8,128)(2,1)} custom-call(bf16[1024,256]{1,0:T(8,128)(2,1)} %bitcast.13, bf16[256,256]{1,0:T(8,128)(2,1)} %shared_ref.5, bf16[256,256]{1,0:T(8,128)(2,1)} %value_ref.5), custom_call_target="tpu_custom_call" | custom-call | flops 268435456 | bytes 1572864 | tf_op jit(solution)/shard_map/project/pallas_call | solution.py:58
  4.7 3.8 %all-to-all-start = ((bf16[4,1024,128]{2,1,0:T(8,128)(2,1)}), bf16[4,1024,128]{2,1,0:T(8,128)(2,1)S(1)}, u32[]{:S(2)}, u32[]{:S(2)}) async-start(bf16[4,1024,128]{2,1,0:T(8,128)(2,1)} %project.3), calls=%async_computation | async-start | bytes 2097152 | tf_op jit(solution)/shard_map/all_to_all | solution.py:34
  8.5 0.5 collective-permute-start.2
  9.0 13.2 %all-to-all-done.own_hbm = bf16[4,1024,128]{2,1,0:T(8,128)(2,1)S(1)} async-done(((bf16[4,1024,128]{2,1,0:T(8,128)(2,1)}), bf16[4,1024,128]{2,1,0:T(8,128)(2,1)S(1)}, u32[]{:S(2)}, u32[]{:S(2)}) %all-to-all-start) | async-done | bytes 1048608 | tf_op jit(solution)/shard_map/all_to_all | solution.py:34
  22.2 0.0 collective-permute-start.1
  22.2 0.0 collective-permute-done.2
  22.2 0.8 copy-done.14
  23.1 2.6 %project.5 = bf16[4,1024,128]{2,1,0:T(8,128)(2,1)} custom-call(bf16[1024,256]{1,0:T(8,128)(2,1)} %bitcast.15, bf16[256,256]{1,0:T(8,128)(2,1)} %shared_ref.5, bf16[256,256]{1,0:T(8,128)(2,1)} %value_ref.5), custom_call_target="tpu_custom_call" | custom-call | flops 13421772800 | bytes 1572864 | tf_op jit(solution)/shard_map/project/pallas_call | solution.py:58
  25.7 3.6 %all-to-all-start.2 = ((bf16[4,1024,128]{2,1,0:T(8,128)(2,1)}), bf16[4,1024,128]{2,1,0:T(8,128)(2,1)S(1)}, u32[]{:S(2)}, u32[]{:S(2)}) async-start(bf16[4,1024,128]{2,1,0:T(8,128)(2,1)} %project.5), calls=%async_computation.2 | async-start | bytes 2097152 | tf_op jit(solution)/shard_map/all_to_all | solution.py:34
  29.4 1.6 %collective-permute-start = (bf16[4,256,256]{2,1,0:T(8,128)(2,1)S(1)}, bf16[4,256,256]{2,1,0:T(8,128)(2,1)S(1)}, u32[]{:S(2)}, u32[]{:S(2)}) collective-permute-start(bf16[4,256,256]{2,1,0:T(8,128)(2,1)S(1)} %copy-done.10), channel_id=1, source_target_pairs={{0,8},{4,28},{8,16},{12,4},{16,24},{20,12},{24,0},{28,20},{1,9},{5... | collective-permute-start | bytes 1572872 | tf_op jit(solution)/shard_map/ppermute | solution.py:317
  31.0 0.1 copy.16
  31.1 0.6 reshape.15.partners
  31.7 14.6 %attend_0.1.refs_0_.after_ref.refs_2_ = f32[2,1024,128]{2,1,0:T(8,128)} custom-call(s32[32]{0:T(128)} %counts.5, s32[64]{0:T(128)} %reshape.15.partners, bf16[4,1024,128]{2,1,0:T(8,128)(2,1)} %copy-done.9, bf16[4,1024,128]{2,1,0:T(8,128)(2,1)} %collective-permute-done.1.refs_0_), custom_call_target="tpu_custom_call" | custom-call | tf_op jit(solution)/shard_map/attend_0/pallas_call | solution.py:254
  46.3 0.0 all-to-all-done.2.value_ref
  46.3 1.0 copy-done.8
  47.3 0.0 collective-permute-start.3
  47.3 0.8 copy-done.13
  48.2 2.6 %project.4 = bf16[4,1024,128]{2,1,0:T(8,128)(2,1)} custom-call(bf16[1024,256]{1,0:T(8,128)(2,1)} %bitcast.14, bf16[256,256]{1,0:T(8,128)(2,1)} %shared_ref.5, bf16[256,256]{1,0:T(8,128)(2,1)} %value_ref.5, f32[2,1024,128]{2,1,0:T(8,128)} %attend_0.1.refs_0_.after_ref.refs_2_), custom_call_target="tpu_custom_call" | custom-call | flops 13421772800 | bytes 1572864 | tf_op jit(solution)/shard_map/project/pallas_call | solution.py:58
  50.8 4.2 %all-to-all-start.1 = ((bf16[4,1024,128]{2,1,0:T(8,128)(2,1)}), bf16[4,1024,128]{2,1,0:T(8,128)(2,1)S(1)}, u32[]{:S(2)}, u32[]{:S(2)}) async-start(bf16[4,1024,128]{2,1,0:T(8,128)(2,1)} %project.4), calls=%async_computation.1 | async-start | bytes 2097152 | tf_op jit(solution)/shard_map/all_to_all | solution.py:34
  54.9 0.0 collective-permute-done.3.refs_1_
  54.9 32.4 %attend_1_3.1.refs_1_ = f32[2,1024,128]{2,1,0:T(8,128)} custom-call(s32[32]{0:T(128)} %counts.5, s32[64]{0:T(128)} %reshape.15.partners, bf16[4,1024,128]{2,1,0:T(8,128)(2,1)} %copy-done.9, bf16[4,1024,128]{2,1,0:T(8,128)(2,1)} %tie.1.refs_0_, bf16[4,1024,128]{2,1,0:T(8,128)(2,1)} %collective-permute-done.3.refs_1_, ...), custom_call_target="tpu_custom_call" | custom-call | flops 17179869184 | bytes 3145728 | tf_op jit(solution)/shard_map/attend_1_3/pallas_call | solution.py:254
  87.3 1.0 copy-done.11
  88.3 0.0 copy-start.6
  88.3 21.7 %attend_2.1 = bf16[4,512,128]{2,1,0:T(8,128)(2,1)} custom-call(s32[32]{0:T(128)} %counts.5, s32[64]{0:T(128)} %reshape.15.partners, bf16[4,1024,128]{2,1,0:T(8,128)(2,1)} %copy-done.9, bf16[4,1024,128]{2,1,0:T(8,128)(2,1)} %copy-done.11, f32[2,1024,128]{2,1,0:T(8,128)} %attend_1_3.1.refs_1_), custom_call_target="tpu_custom_call" | custom-call | flops 8589934592 | bytes 3145728 | tf_op jit(solution)/shard_map/attend_2/pallas_call | solution.py:254
  110.0 0.0 copy-start
  110.0 4.3 %all-to-all-start.3 = ((bf16[4,512,128]{2,1,0:T(8,128)(2,1)}), bf16[4,512,128]{2,1,0:T(8,128)(2,1)S(1)}, u32[]{:S(2)}, u32[]{:S(2)}) async-start(bf16[4,512,128]{2,1,0:T(8,128)(2,1)} %attend_2.1), calls=%async_computation.3 | async-start | bytes 1048576 | tf_op jit(solution)/shard_map/all_to_all | solution.py:34
  114.3 0.1 broadcast_in_dim_reshape.3.everyone
  114.4 6.5 %all-to-all-done.3 = bf16[4,512,128]{2,1,0:T(8,128)(2,1)S(1)} async-done(((bf16[4,512,128]{2,1,0:T(8,128)(2,1)}), bf16[4,512,128]{2,1,0:T(8,128)(2,1)S(1)}, u32[]{:S(2)}, u32[]{:S(2)}) %all-to-all-start.3) | async-done | bytes 524320 | tf_op jit(solution)/shard_map/all_to_all | solution.py:34
  121.0 0.6 copy-done.4
  121.6 0.0 copy-done.7
  121.6 3.4 %refine.1 = f32[4,256,256]{2,1,0:T(8,128)} custom-call(s32[1,64]{1,0:T(1,128)S(1)} %broadcast_in_dim_reshape.3.everyone, f32[4,256,256]{2,1,0:T(8,128)S(1)} %copy-done, bf16[4,2,256,128]{3,2,1,0:T(8,128)(2,1)S(1)} %bitcast.8, bf16[256,256]{1,0:T(8,128)(2,1)S(1)} %copy-done.3, bf16[512,512]{1,0:T(8,128)(2,1)S(1)} %copy-done.1, f32[1,512]{1,0:T(1,128)S(1)} %bitcast.9, ...), custom_call_target="tpu_custom_call" | custom-call | flops 1342177280 | bytes 4194304 | tf_op jit(solution)/shard_map/refine/pallas_call | solution.py:334
  (26 shorter events, 0.0 us)
Async XLA Ops:
  4.7 3.8 %copy-start.10 = (bf16[4,256,256]{2,1,0:T(8,128)(2,1)S(1)}, bf16[4,256,256]{2,1,0:T(8,128)(2,1)}, u32[]{:S(2)}) copy-start(bf16[4,256,256]{2,1,0:T(8,128)(2,1)} %convert_element_type.3) | copy-start | bytes 1572868
  4.7 17.5 %all-to-all-start = ((bf16[4,1024,128]{2,1,0:T(8,128)(2,1)}), bf16[4,1024,128]{2,1,0:T(8,128)(2,1)S(1)}, u32[]{:S(2)}, u32[]{:S(2)}) async-start(bf16[4,1024,128]{2,1,0:T(8,128)(2,1)} %project.3), calls=%async_computation | async-start | bytes 2097152 | tf_op jit(solution)/shard_map/all_to_all | solution.py:34
  8.5 13.7 %collective-permute-start.2 = (bf16[4,256,256]{2,1,0:T(8,128)(2,1)S(1)}, bf16[4,256,256]{2,1,0:T(8,128)(2,1)S(1)}, u32[]{:S(2)}, u32[]{:S(2)}) collective-permute-start(bf16[4,256,256]{2,1,0:T(8,128)(2,1)S(1)} %copy-done.10), channel_id=1, source_target_pairs={{0,24},{4,12},{8,0},{12,20},{16,8},{20,28},{24,16},{28,4},{1,25},{... | collective-permute-start | bytes 1572872 | tf_op jit(solution)/shard_map/ppermute | solution.py:316
  22.2 3.5 %copy-start.9 = (bf16[4,1024,128]{2,1,0:T(8,128)(2,1)}, bf16[4,1024,128]{2,1,0:T(8,128)(2,1)S(1)}, u32[]{:S(2)}) copy-start(bf16[4,1024,128]{2,1,0:T(8,128)(2,1)S(1)} %all-to-all-done.own_hbm) | copy-start | bytes 3145732
  22.2 9.5 %collective-permute-start.1 = (bf16[4,1024,128]{2,1,0:T(8,128)(2,1)S(1)}, bf16[4,1024,128]{2,1,0:T(8,128)(2,1)}, u32[]{:S(2)}, u32[]{:S(2)}) collective-permute-start(bf16[4,1024,128]{2,1,0:T(8,128)(2,1)S(1)} %all-to-all-done.own_hbm), channel_id=1, source_target_pairs={{0,4},{4,0},{8,12},{12,8},{16,20},{20,16},{24,28},{28,24},{1,5},{5... | collective-permute-start | bytes 3145736 | tf_op jit(solution)/shard_map/ppermute | solution.py:322
  22.2 0.9 copy-start.14
  25.7 5.3 %copy-start.12 = (s32[32,2]{0,1:T(2,128)S(1)}, s32[32,2]{0,1:T(2,128)}, u32[]{:S(2)}) copy-start(s32[32,2]{0,1:T(2,128)} %param.13) | copy-start | bytes 772
  25.7 20.6 %all-to-all-start.2 = ((bf16[4,1024,128]{2,1,0:T(8,128)(2,1)}), bf16[4,1024,128]{2,1,0:T(8,128)(2,1)S(1)}, u32[]{:S(2)}, u32[]{:S(2)}) async-start(bf16[4,1024,128]{2,1,0:T(8,128)(2,1)} %project.5), calls=%async_computation.2 | async-start | bytes 2097152 | tf_op jit(solution)/shard_map/all_to_all | solution.py:34
  29.4 18.0 %collective-permute-start = (bf16[4,256,256]{2,1,0:T(8,128)(2,1)S(1)}, bf16[4,256,256]{2,1,0:T(8,128)(2,1)S(1)}, u32[]{:S(2)}, u32[]{:S(2)}) collective-permute-start(bf16[4,256,256]{2,1,0:T(8,128)(2,1)S(1)} %copy-done.10), channel_id=1, source_target_pairs={{0,8},{4,28},{8,16},{12,4},{16,24},{20,12},{24,0},{28,20},{1,9},{5... | collective-permute-start | bytes 1572872 | tf_op jit(solution)/shard_map/ppermute | solution.py:317
  46.3 1.0 copy-start.8
  47.3 7.6 %collective-permute-start.3 = (bf16[4,1024,128]{2,1,0:T(8,128)(2,1)}, bf16[4,1024,128]{2,1,0:T(8,128)(2,1)}, u32[]{:S(2)}, u32[]{:S(2)}) collective-permute-start(bf16[4,1024,128]{2,1,0:T(8,128)(2,1)} %tie.1.refs_0_), channel_id=1, source_target_pairs={{0,4},{4,0},{8,12},{12,8},{16,20},{20,16},{24,28},{28,24},{1,5},{5... | collective-permute-start | bytes 3145736 | tf_op jit(solution)/shard_map/ppermute | solution.py:327
  47.3 0.8 copy-start.13
  50.8 36.5 %all-to-all-start.1 = ((bf16[4,1024,128]{2,1,0:T(8,128)(2,1)}), bf16[4,1024,128]{2,1,0:T(8,128)(2,1)S(1)}, u32[]{:S(2)}, u32[]{:S(2)}) async-start(bf16[4,1024,128]{2,1,0:T(8,128)(2,1)} %project.4), calls=%async_computation.1 | async-start | bytes 2097152 | tf_op jit(solution)/shard_map/all_to_all | solution.py:34
  87.3 1.0 copy-start.11
  88.3 32.6 %copy-start.1 = (bf16[512,512]{1,0:T(8,128)(2,1)S(1)}, bf16[512,512]{1,0:T(8,128)(2,1)}, u32[]{:S(2)}) copy-start(bf16[512,512]{1,0:T(8,128)(2,1)} %ffn_in.1) | copy-start | bytes 1572868
  88.3 32.6 %copy-start.2 = (bf16[512,256]{1,0:T(8,128)(2,1)S(1)}, bf16[512,256]{1,0:T(8,128)(2,1)}, u32[]{:S(2)}) copy-start(bf16[512,256]{1,0:T(8,128)(2,1)} %ffn_out.1) | copy-start | bytes 786436
  88.3 32.6 %copy-start.3 = (bf16[256,256]{1,0:T(8,128)(2,1)S(1)}, bf16[256,256]{1,0:T(8,128)(2,1)}, u32[]{:S(2)}) copy-start(bf16[256,256]{1,0:T(8,128)(2,1)} %out_proj.1) | copy-start | bytes 393220
  88.3 32.6 %copy-start.5 = (f32[512]{0:T(512)S(1)}, f32[512]{0:T(512)}, u32[]{:S(2)}) copy-start(f32[512]{0:T(512)} %param.20) | copy-start | bytes 6148
  88.3 32.6 %copy-start.6 = (f32[512]{0:T(512)S(1)}, f32[512]{0:T(512)}, u32[]{:S(2)}) copy-start(f32[512]{0:T(512)} %param.21) | copy-start | bytes 6148
  110.0 11.0 %copy-start = (f32[4,256,256]{2,1,0:T(8,128)S(1)}, f32[4,256,256]{2,1,0:T(8,128)}, u32[]{:S(2)}) copy-start(f32[4,256,256]{2,1,0:T(8,128)} %features.1) | copy-start | bytes 3145732
  110.0 10.9 %all-to-all-start.3 = ((bf16[4,512,128]{2,1,0:T(8,128)(2,1)}), bf16[4,512,128]{2,1,0:T(8,128)(2,1)S(1)}, u32[]{:S(2)}, u32[]{:S(2)}) async-start(bf16[4,512,128]{2,1,0:T(8,128)(2,1)} %attend_2.1), calls=%async_computation.3 | async-start | bytes 1048576 | tf_op jit(solution)/shard_map/all_to_all | solution.py:34
  120.9 0.7 copy-start.4
  120.9 0.7 copy-start.7
where the time goes:
time: 127 us; the launch traced here: 125 us
  Pallas kernels  79.8 us (63%)
  waiting for transfers between devices  19.7 us (16%)
  starting transfers between devices  18 us (14%)
  local copies, waits for them, and re-layouts  5.17 us (4%)
  other arithmetic  2.07 us (2%)
    pallas_call x3, Pallas kernels, attend(): pl.pallas_call(functools.partial(attend_kernel, kinds, first, last, head_...  68.6 us
    all_to_all x4, waiting for transfers between devices, exchange(): return lax.all_to_all(value, 'row', split_axis=0, concat_axis=0, tiled=True)  19.7 us
    all_to_all x4, starting transfers between devices, exchange(): return lax.all_to_all(value, 'row', split_axis=0, concat_axis=0, tiled=True)  16 us
    pallas_call x3, Pallas kernels, project(): pl.pallas_call(kernel, out_shape=jax.ShapeDtypeStruct((HEADS, rows, 2 * h...  7.83 us
    unnamed x31, local copies, waits for them, and re-layouts  4.44 us
    pallas_call x1, Pallas kernels, per_device(): pl.pallas_call(functools.partial(refine_kernel, head_dim), grid=(per_dev...  3.36 us
  transfers between devices with their start and end apart: 8, of which 2 were waited for; matrix products, arithmetic and copies ran while one was open for 1% of the time, Pallas kernels for 42%

commit v1 on v0

--- a/solution.py
+++ b/solution.py
@@ -34,14 +34,18 @@
     return lax.all_to_all(value, "row", split_axis=0, concat_axis=0, tiled=True)
 
 
-def project_kernel(head_dim, rows, shared_proj, value_proj, out):
+def project_kernel(head_dim, rounds, rows, shared_proj, value_proj, *outs):
+    out = outs[-1]
     heads, _, lanes = out.shape
     low = lax.broadcasted_iota(jnp.int32, (1, lanes), 1) < head_dim
+    source = rows[...].astype(BF16)
+    if rounds:
+        outs[0][...] = source
     for pair in range(heads // 2):
         columns = slice(pair * lanes, (pair + 1) * lanes)
         turned = pltpu.roll(value_proj[:, columns].astype(F32), head_dim, 1).astype(BF16)
         both = jnp.concatenate([shared_proj[:, columns], turned], axis=1)
-        projected = jnp.dot(rows[...], both, preferred_element_type=F32)
+        projected = jnp.dot(source, both, preferred_element_type=F32)
         shared, values = projected[:, :lanes], projected[:, lanes:]
         out[2 * pair] = jnp.where(low, shared, values).astype(BF16)
         out[2 * pair + 1] = jnp.where(low, values, shared).astype(BF16)
@@ -51,15 +55,23 @@
     per_dev, row_count, width = value.shape
     rows = per_dev * row_count
     head_dim = width // HEADS
+    rounds = value.dtype == F32
 
     def kernel(rows_ref, shared_ref, value_ref, *refs):
-        project_kernel(head_dim, rows_ref, shared_ref, value_ref, refs[-1])
-
-    packed = pl.pallas_call(
+        project_kernel(head_dim, rounds, rows_ref, shared_ref, value_ref, *refs[len(after):])
+
+    part = pl.BlockSpec((row_count, width), lambda i: (i, 0))
+    out_shapes = [jax.ShapeDtypeStruct((HEADS, rows, 2 * head_dim), BF16)]
+    out_specs = [pl.BlockSpec((HEADS, row_count, 2 * head_dim), lambda i: (0, i, 0))]
+    if rounds:
+        out_shapes.insert(0, jax.ShapeDtypeStruct((rows, width), BF16))
+        out_specs.insert(0, part)
+    *rounded, packed = pl.pallas_call(
         kernel,
-        out_shape=jax.ShapeDtypeStruct((HEADS, rows, 2 * head_dim), BF16),
-        in_specs=[whole()] * 3 + [whole(pl.ANY)] * len(after),
-        out_specs=whole(),
+        grid=(per_dev,),
+        out_shape=out_shapes,
+        in_specs=[part] + [whole()] * 2 + [whole(pl.ANY)] * len(after),
+        out_specs=out_specs,
         compiler_params=pltpu.CompilerParams(vmem_limit_bytes=VMEM),
         cost_estimate=pl.CostEstimate(
             flops=weigh * 4 * rows * width * width, bytes_accessed=6 * rows * width, transcendentals=0
@@ -68,7 +80,8 @@
     )(value.reshape(rows, width), shared_proj, value_proj, *after)
     if row_devices > HEADS:
         packed = jnp.repeat(packed, row_devices // HEADS, axis=0)
-    return exchange(packed)
+    packed = exchange(packed)
+    return (rounded[0].reshape(value.shape), packed) if rounds else packed
 
 
 def tie(value, after):
@@ -88,9 +101,9 @@
 def attend_kernel(kinds, first, last, head_dim, counts, partners, own_hbm, *refs):
     blocks_hbm, refs = refs[:len(kinds)], refs[len(kinds):]
     if first:
-        out_hbm, own, blocks, total, limits, todo, arrived, out, left = refs
+        out_hbm, own, blocks, keys, values, turned, total, limits, todo, arrived, out, left = refs
     else:
-        carried_hbm, out_hbm, own, blocks, total, limits, todo, arrived, out, left, carried, carried_here = refs
+        carried_hbm, out_hbm, own, blocks, keys, values, turned, total, limits, todo, arrived, out, left, carried, carried_here = refs
     devices, flat_rows, lanes = own.shape
     img_count = lax.axis_size("img")
     me = lax.axis_index("img")
@@ -144,48 +157,54 @@
     def image_rows(image):
         return pl.ds(pl.multiple_of(image * row_count, row_count), row_count)
 
-    def operands(number):
-        other, image, limit = todo[0, number], todo[1, number], todo[3, number]
-        place, other = lax.div(other, per_dev), lax.rem(other, per_dev)
-        tile = blocks[place, :, image_rows(other), :].reshape(keypoints, lanes)
-        is_key, present = lane_side == key_side, key_row < limit
-        keys = jnp.where(present, jnp.where(is_key, tile, zero), zero)
-        values = jnp.where(present, jnp.where(is_key, one, tile), zero)
-        return image, keys, values, limit, todo[2, number].astype(F32)
-
-    def score(image, start, keys):
+    value_rows = pl.ds(pl.multiple_of((1 - key_side) * head_dim, head_dim), head_dim)
+    for place, kind in enumerate(kinds):
+        block_id = block_of(kind, me, img_count)
+        for other in range(per_dev):
+            spot = place * per_dev + other
+            limit = counts[block_id * per_dev + other]
+            tile = blocks[place, :, other * row_count:(other + 1) * row_count].reshape(keypoints, lanes)
+            keys[spot] = jnp.where(key_row < limit, jnp.where(lane_side == key_side, tile, zero), zero)
+            turned[...] = tile.T
+            values[spot, :head_dim] = jnp.where(key_lane < limit, turned[value_rows], zero)
+            values[spot, head_dim:] = jnp.broadcast_to(
+                jnp.where(key_lane < limit, one, zero), (values.shape[1] - head_dim, keypoints)
+            )
+
+    def score(spot, image, start):
         queries = own[start:start + sources, image_rows(image), :].reshape(once, lanes)
-        return lax.dot_general(queries, keys, NT, preferred_element_type=F32)
+        return lax.dot_general(keys[spot], queries, NT, preferred_element_type=F32)
 
     def add(image, start, got, times):
-        rows = slice(start * row_count, start * row_count + once)
-        total[image, rows] += got * times / pltpu.roll(got, head_dim, 1)
+        columns = slice(start * row_count, start * row_count + once)
+        share = times / got[head_dim:head_dim + 8]
+        messages = got[:head_dim].reshape(head_dim // 8, 8, once) * share
+        total[image, :, columns] += messages.reshape(head_dim, once)
 
     def fast(numbers):
-        work = [operands(number) for number in numbers]
+        work = [(todo[0, number], todo[1, number], todo[2, number].astype(F32)) for number in numbers]
         least, most = limits[0], limits[1]
         for start in range(0, devices, sources):
             results = []
-            for image, keys, values, _, times in work:
-                raised = jnp.exp2(score(image, start, keys) * factor).astype(BF16)
-                got = jnp.dot(raised, values, preferred_element_type=F32)
-                by_row = got.reshape(once // 8, 8, lanes)
-                least = jnp.minimum(least, jnp.min(by_row, axis=0))
-                most = jnp.maximum(most, jnp.max(by_row, axis=0))
+            for spot, image, _ in work:
+                raised = jnp.exp2(score(spot, image, start) * factor).astype(BF16)
+                got = jnp.dot(values[spot], raised, preferred_element_type=F32)
+                least = jnp.minimum(least, got[head_dim:head_dim + 8])
+                most = jnp.maximum(most, got[head_dim:head_dim + 8])
                 results.append(got)
-            for (image, _, _, _, times), got in zip(work, results):
+            for (_, image, times), got in zip(work, results):
                 add(image, start, got, times)
         limits[0] = least
         limits[1] = most
 
     def slow(number, carry):
-        image, keys, values, limit, times = operands(number)
-        present = key_lane < limit
+        spot, image, times = todo[0, number], todo[1, number], todo[2, number].astype(F32)
+        present = key_row < todo[3, number]
         for start in range(0, devices, sources):
-            scores = score(image, start, keys)
-            peak = jnp.max(jnp.where(present, scores, NEGATIVE), axis=1, keepdims=True)
+            scores = score(spot, image, start)
+            peak = jnp.max(jnp.where(present, scores, NEGATIVE), axis=0, keepdims=True)
             raised = jnp.where(present, jnp.exp2((scores - peak) * factor), 0.0).astype(BF16)
-            add(image, start, jnp.dot(raised, values, preferred_element_type=F32), times)
+            add(image, start, jnp.dot(values[spot], raised, preferred_element_type=F32), times)
         return carry
 
     def two(number, carry):
@@ -199,9 +218,8 @@
         fast((pairs - 1,))
 
     outside = (limits[0] < LEAST) | (limits[1] > MOST)
-    outside = jnp.where((lane_side == key_side) & outside, 1.0, 0.0)
-
-    @pl.when(jnp.max(outside) > 0.5)
+
+    @pl.when(jnp.max(jnp.where(outside, 1.0, 0.0)) > 0.5)
     def _():
         total[...] = jnp.zeros_like(total)
         lax.fori_loop(0, pairs, slow, 0)
@@ -210,10 +228,7 @@
         carry_copy.wait()
     gone = []
     for pair in range(per_dev // 2):
-        even, uneven = total[2 * pair], total[2 * pair + 1]
-        even_low = jnp.where(key_side == 1, even, pltpu.roll(even, head_dim, 1))
-        uneven_high = jnp.where(key_side == 0, uneven, pltpu.roll(uneven, head_dim, 1))
-        both = jnp.where(lane_side == 0, even_low, uneven_high)
+        both = total[2 * pair:2 * pair + 2].reshape(lanes, keypoints).T
         if not first:
             both += carried[pair]
         if last:
@@ -242,8 +257,11 @@
     scratch = [
         pltpu.VMEM(own.shape, BF16),
         pltpu.VMEM((len(kinds), *own.shape), BF16),
-        pltpu.VMEM((per_dev, keypoints, lanes), F32),
-        pltpu.VMEM((2, 8, lanes), F32),
+        pltpu.VMEM((len(kinds) * per_dev, keypoints, lanes), BF16),
+        pltpu.VMEM((len(kinds) * per_dev, head_dim + 16, keypoints), BF16),
+        pltpu.VMEM((lanes, keypoints), BF16),
+        pltpu.VMEM((per_dev, head_dim, keypoints), F32),
+        pltpu.VMEM((2, 8, max(256, flat_rows // per_dev)), F32),
         pltpu.SMEM((4, len(kinds) * per_dev * per_dev + 1), jnp.int32),
         pltpu.SemaphoreType.DMA((1 + len(kinds), devices)),
         pltpu.VMEM(out_shape.shape, out_shape.dtype),
@@ -312,13 +330,12 @@
     thick_pairs = [(s, (s + (2 if s % 2 else -2)) % img_count) for s in blocks]
     thin_pairs = [(s, (s + (-2 if s % 2 else 2)) % img_count) for s in blocks]
 
-    rounded = features.astype(BF16)
+    weights = (shared_proj, value_proj, row_devices)
+    rounded, own = project(features, *weights)
     thick = lax.ppermute(rounded, "img", thick_pairs)
     thin = lax.ppermute(rounded, "img", thin_pairs)
     flat_partners = partners.reshape(-1)
 
-    weights = (shared_proj, value_proj, row_devices)
-    own = project(rounded, *weights)
     companion = lax.ppermute(own, "img", swap)
     thick = project(thick, *weights, weigh=50)
     work = functools.partial(attend, head_dim=head_dim, counts=counts, partners=flat_partners, own=own)

time: 127 us -> 155 us (1.22)
  the two profiles are of different devices: /device:TPU:16 before, /device:TPU:8 now
where the time goes in v1:
time: 155 us; the launch traced here: 153 us
  Pallas kernels  109 us (70%)
  waiting for transfers between devices  20.4 us (13%)
  starting transfers between devices  17.4 us (11%)
  local copies, waits for them, and re-layouts  6.34 us (4%)
    pallas_call x3, Pallas kernels, attend(): pl.pallas_call(functools.partial(attend_kernel, kinds, first, last, head_...  93.3 us
    all_to_all x4, waiting for transfers between devices, exchange(): return lax.all_to_all(value, 'row', split_axis=0, concat_axis=0, tiled=True)  19.7 us
    all_to_all x4, starting transfers between devices, exchange(): return lax.all_to_all(value, 'row', split_axis=0, concat_axis=0, tiled=True)  16.2 us
    pallas_call x3, Pallas kernels, project(): pl.pallas_call(kernel, grid=(per_dev,), out_shape=out_shapes, in_specs=[p...  12 us
    unnamed x33, local copies, waits for them, and re-layouts  5.54 us
    pallas_call x1, Pallas kernels, per_device(): pl.pallas_call(functools.partial(refine_kernel, head_dim), grid=(per_dev...  3.36 us
  transfers between devices with their start and end apart: 8, of which 3 were waited for; matrix products, arithmetic and copies ran while one was open for 1% of the time, Pallas kernels for 51%

profile of v1, /device:TPU:8, one launch (start us, length us, event | category | flops | bytes accessed | tf_op | source)
XLA Modules:
  0.0 153.0 jit_solution(4294947743841880922)
XLA Ops:
  0.0 4.0 %project.3 = (bf16[1024,256]{1,0:T(8,128)(2,1)}, bf16[4,1024,128]{2,1,0:T(8,128)(2,1)}) custom-call(f32[1024,256]{1,0:T(8,128)} %bitcast.9, bf16[256,256]{1,0:T(8,128)(2,1)} %shared_ref.5, bf16[256,256]{1,0:T(8,128)(2,1)} %value_ref.5), custom_call_target="tpu_custom_call" | custom-call | flops 268435456 | bytes 1572864 | tf_op jit(solution)/shard_map/project/pallas_call | solution.py:69
  4.0 3.8 %all-to-all-start = ((bf16[4,1024,128]{2,1,0:T(8,128)(2,1)}), bf16[4,1024,128]{2,1,0:T(8,128)(2,1)S(1)}, u32[]{:S(2)}, u32[]{:S(2)}) async-start(bf16[4,1024,128]{2,1,0:T(8,128)(2,1)} %get-tuple-element.7), calls=%async_computation | async-start | bytes 2097152 | tf_op jit(solution)/shard_map/all_to_all | solution.py:34
  7.9 0.5 collective-permute-start.2
  8.3 13.2 %all-to-all-done.own_hbm = bf16[4,1024,128]{2,1,0:T(8,128)(2,1)S(1)} async-done(((bf16[4,1024,128]{2,1,0:T(8,128)(2,1)}), bf16[4,1024,128]{2,1,0:T(8,128)(2,1)S(1)}, u32[]{:S(2)}, u32[]{:S(2)}) %all-to-all-start) | async-done | bytes 1048608 | tf_op jit(solution)/shard_map/all_to_all | solution.py:34
  21.6 0.0 collective-permute-start.1
  21.6 0.7 collective-permute-done.2
  22.3 0.8 copy-done.15
  23.1 4.0 %project.5 = bf16[4,1024,128]{2,1,0:T(8,128)(2,1)} custom-call(bf16[1024,256]{1,0:T(8,128)(2,1)} %bitcast.17, bf16[256,256]{1,0:T(8,128)(2,1)} %shared_ref.5, bf16[256,256]{1,0:T(8,128)(2,1)} %value_ref.5), custom_call_target="tpu_custom_call" | custom-call | flops 13421772800 | bytes 1572864 | tf_op jit(solution)/shard_map/project/pallas_call | solution.py:69
  27.1 4.0 %all-to-all-start.2 = ((bf16[4,1024,128]{2,1,0:T(8,128)(2,1)}), bf16[4,1024,128]{2,1,0:T(8,128)(2,1)S(1)}, u32[]{:S(2)}, u32[]{:S(2)}) async-start(bf16[4,1024,128]{2,1,0:T(8,128)(2,1)} %project.5), calls=%async_computation.2 | async-start | bytes 2097152 | tf_op jit(solution)/shard_map/all_to_all | solution.py:34
  31.0 0.7 collective-permute-start
  31.7 0.1 copy.16
  31.8 0.7 reshape.18.partners
  32.5 0.0 collective-permute-done.1.refs_0_
  32.5 1.0 copy-done.10
  33.5 32.3 %attend_0.1.refs_0_.after_ref.refs_2_ = f32[2,1024,128]{2,1,0:T(8,128)} custom-call(s32[32]{0:T(128)} %counts.5, s32[64]{0:T(128)} %reshape.18.partners, bf16[4,1024,128]{2,1,0:T(8,128)(2,1)} %copy-done.9, bf16[4,1024,128]{2,1,0:T(8,128)(2,1)} %copy-done.10), custom_call_target="tpu_custom_call" | custom-call | tf_op jit(solution)/shard_map/attend_0/pallas_call | solution.py:272
  65.9 1.0 copy-done.8
  66.9 0.0 collective-permute-start.3
  66.9 4.0 %project.4 = bf16[4,1024,128]{2,1,0:T(8,128)(2,1)} custom-call(bf16[1024,256]{1,0:T(8,128)(2,1)} %bitcast.2.rows_ref, bf16[256,256]{1,0:T(8,128)(2,1)} %shared_ref.5, bf16[256,256]{1,0:T(8,128)(2,1)} %value_ref.5, f32[2,1024,128]{2,1,0:T(8,128)} %attend_0.1.refs_0_.after_ref.refs_2_), custom_call_target="tpu_custom_call" | custom-call | flops 13421772800 | bytes 1572864 | tf_op jit(solution)/shard_map/project/pallas_call | solution.py:69
  70.9 4.1 %all-to-all-start.1 = ((bf16[4,1024,128]{2,1,0:T(8,128)(2,1)}), bf16[4,1024,128]{2,1,0:T(8,128)(2,1)S(1)}, u32[]{:S(2)}, u32[]{:S(2)}) async-start(bf16[4,1024,128]{2,1,0:T(8,128)(2,1)} %project.4), calls=%async_computation.1 | async-start | bytes 2097152 | tf_op jit(solution)/shard_map/all_to_all | solution.py:34
  75.0 0.0 collective-permute-done.3.refs_1_
  75.0 1.0 copy-done.13
  76.0 38.0 %attend_1_3.1.refs_1_ = f32[2,1024,128]{2,1,0:T(8,128)} custom-call(s32[32]{0:T(128)} %counts.5, s32[64]{0:T(128)} %reshape.18.partners, bf16[4,1024,128]{2,1,0:T(8,128)(2,1)} %copy-done.9, bf16[4,1024,128]{2,1,0:T(8,128)(2,1)} %tie.1.refs_0_, bf16[4,1024,128]{2,1,0:T(8,128)(2,1)} %copy-done.13, f32[2,1024,128]{2,1,0:T(8,128)} %attend_0.1.refs_0_.after_ref.refs_2_), custom_call_target="tpu_custom_call" | custom-call | flops 17179869184 | bytes 3145728 | tf_op jit(solution)/shard_map/attend_1_3/pallas_call | solution.py:272
  114.0 1.0 copy-done.11
  115.0 0.0 copy-start.6
  115.0 22.9 %attend_2.1 = bf16[4,512,128]{2,1,0:T(8,128)(2,1)} custom-call(s32[32]{0:T(128)} %counts.5, s32[64]{0:T(128)} %reshape.18.partners, bf16[4,1024,128]{2,1,0:T(8,128)(2,1)} %copy-done.9, bf16[4,1024,128]{2,1,0:T(8,128)(2,1)} %copy-done.11, f32[2,1024,128]{2,1,0:T(8,128)} %attend_1_3.1.refs_1_), custom_call_target="tpu_custom_call" | custom-call | flops 8589934592 | bytes 3145728 | tf_op jit(solution)/shard_map/attend_2/pallas_call | solution.py:272
  138.0 0.0 copy-start
  138.0 4.3 %all-to-all-start.3 = ((bf16[4,512,128]{2,1,0:T(8,128)(2,1)}), bf16[4,512,128]{2,1,0:T(8,128)(2,1)S(1)}, u32[]{:S(2)}, u32[]{:S(2)}) async-start(bf16[4,512,128]{2,1,0:T(8,128)(2,1)} %attend_2.1), calls=%async_computation.3 | async-start | bytes 1048576 | tf_op jit(solution)/shard_map/all_to_all | solution.py:34
  142.3 0.1 broadcast_in_dim_reshape.3.everyone
  142.4 6.5 %all-to-all-done.3 = bf16[4,512,128]{2,1,0:T(8,128)(2,1)S(1)} async-done(((bf16[4,512,128]{2,1,0:T(8,128)(2,1)}), bf16[4,512,128]{2,1,0:T(8,128)(2,1)S(1)}, u32[]{:S(2)}, u32[]{:S(2)}) %all-to-all-start.3) | async-done | bytes 524320 | tf_op jit(solution)/shard_map/all_to_all | solution.py:34
  148.9 0.6 copy-done.4
  149.6 0.0 copy-done.7
  149.6 3.4 %refine.1 = f32[4,256,256]{2,1,0:T(8,128)} custom-call(s32[1,64]{1,0:T(1,128)S(1)} %broadcast_in_dim_reshape.3.everyone, f32[4,256,256]{2,1,0:T(8,128)S(1)} %copy-done, bf16[4,2,256,128]{3,2,1,0:T(8,128)(2,1)S(1)} %bitcast.10, bf16[256,256]{1,0:T(8,128)(2,1)S(1)} %copy-done.3, bf16[512,512]{1,0:T(8,128)(2,1)S(1)} %copy-done.1, f32[1,512]{1,0:T(1,128)S(1)} %bitcast.11, ...), custom_call_target="tpu_custom_call" | custom-call | flops 1342177280 | bytes 4194304 | tf_op jit(solution)/shard_map/refine/pallas_call | solution.py:351
  (27 shorter events, 0.1 us)
Async XLA Ops:
  4.0 3.8 %copy-start.14 = (bf16[1024,256]{1,0:T(8,128)(2,1)S(1)}, bf16[1024,256]{1,0:T(8,128)(2,1)}, u32[]{:S(2)}) copy-start(bf16[1024,256]{1,0:T(8,128)(2,1)} %get-tuple-element.8) | copy-start | bytes 1572868
  4.0 17.5 %all-to-all-start = ((bf16[4,1024,128]{2,1,0:T(8,128)(2,1)}), bf16[4,1024,128]{2,1,0:T(8,128)(2,1)S(1)}, u32[]{:S(2)}, u32[]{:S(2)}) async-start(bf16[4,1024,128]{2,1,0:T(8,128)(2,1)} %get-tuple-element.7), calls=%async_computation | async-start | bytes 2097152 | tf_op jit(solution)/shard_map/all_to_all | solution.py:34
  7.9 14.4 %collective-permute-start.2 = (bf16[4,256,256]{2,1,0:T(8,128)(2,1)S(1)}, bf16[4,256,256]{2,1,0:T(8,128)(2,1)S(1)}, u32[]{:S(2)}, u32[]{:S(2)}) collective-permute-start(bf16[4,256,256]{2,1,0:T(8,128)(2,1)S(1)} %bitcast.16), channel_id=1, source_target_pairs={{0,24},{4,12},{8,0},{12,20},{16,8},{20,28},{24,16},{28,4},{1,25},{... | collective-permute-start | bytes 1572872 | tf_op jit(solution)/shard_map/ppermute | solution.py:335
  21.6 5.5 %copy-start.9 = (bf16[4,1024,128]{2,1,0:T(8,128)(2,1)}, bf16[4,1024,128]{2,1,0:T(8,128)(2,1)S(1)}, u32[]{:S(2)}) copy-start(bf16[4,1024,128]{2,1,0:T(8,128)(2,1)S(1)} %all-to-all-done.own_hbm) | copy-start | bytes 3145732
  21.6 11.0 %collective-permute-start.1 = (bf16[4,1024,128]{2,1,0:T(8,128)(2,1)S(1)}, bf16[4,1024,128]{2,1,0:T(8,128)(2,1)S(1)}, u32[]{:S(2)}, u32[]{:S(2)}) collective-permute-start(bf16[4,1024,128]{2,1,0:T(8,128)(2,1)S(1)} %all-to-all-done.own_hbm), channel_id=1, source_target_pairs={{0,4},{4,0},{8,12},{12,8},{16,20},{20,16},{24,28},{28,24},{1,5},{5... | collective-permute-start | bytes 3145736 | tf_op jit(solution)/shard_map/ppermute | solution.py:339
  22.3 0.8 copy-start.15
  27.1 4.7 %copy-start.12 = (s32[32,2]{0,1:T(2,128)S(1)}, s32[32,2]{0,1:T(2,128)}, u32[]{:S(2)}) copy-start(s32[32,2]{0,1:T(2,128)} %param.13) | copy-start | bytes 772
  27.1 38.8 %all-to-all-start.2 = ((bf16[4,1024,128]{2,1,0:T(8,128)(2,1)}), bf16[4,1024,128]{2,1,0:T(8,128)(2,1)S(1)}, u32[]{:S(2)}, u32[]{:S(2)}) async-start(bf16[4,1024,128]{2,1,0:T(8,128)(2,1)} %project.5), calls=%async_computation.2 | async-start | bytes 2097152 | tf_op jit(solution)/shard_map/all_to_all | solution.py:34
  31.0 35.9 %collective-permute-start = (bf16[4,256,256]{2,1,0:T(8,128)(2,1)}, bf16[4,256,256]{2,1,0:T(8,128)(2,1)}, u32[]{:S(2)}, u32[]{:S(2)}) collective-permute-start(bf16[4,256,256]{2,1,0:T(8,128)(2,1)} %bitcast.15), channel_id=1, source_target_pairs={{0,8},{4,28},{8,16},{12,4},{16,24},{20,12},{24,0},{28,20},{1,9},{5... | collective-permute-start | bytes 1572872 | tf_op jit(solution)/shard_map/ppermute | solution.py:336
  32.5 1.0 copy-start.10
  65.9 1.0 copy-start.8
  66.9 8.1 %collective-permute-start.3 = (bf16[4,1024,128]{2,1,0:T(8,128)(2,1)}, bf16[4,1024,128]{2,1,0:T(8,128)(2,1)S(1)}, u32[]{:S(2)}, u32[]{:S(2)}) collective-permute-start(bf16[4,1024,128]{2,1,0:T(8,128)(2,1)} %tie.1.refs_0_), channel_id=1, source_target_pairs={{0,4},{4,0},{8,12},{12,8},{16,20},{20,16},{24,28},{28,24},{1,5},{5... | collective-permute-start | bytes 3145736 | tf_op jit(solution)/shard_map/ppermute | solution.py:344
  70.9 43.1 %all-to-all-start.1 = ((bf16[4,1024,128]{2,1,0:T(8,128)(2,1)}), bf16[4,1024,128]{2,1,0:T(8,128)(2,1)S(1)}, u32[]{:S(2)}, u32[]{:S(2)}) async-start(bf16[4,1024,128]{2,1,0:T(8,128)(2,1)} %project.4), calls=%async_computation.1 | async-start | bytes 2097152 | tf_op jit(solution)/shard_map/all_to_all | solution.py:34
  75.0 1.0 copy-start.13
  114.0 1.0 copy-start.11
  115.0 33.9 %copy-start.1 = (bf16[512,512]{1,0:T(8,128)(2,1)S(1)}, bf16[512,512]{1,0:T(8,128)(2,1)}, u32[]{:S(2)}) copy-start(bf16[512,512]{1,0:T(8,128)(2,1)} %ffn_in.1) | copy-start | bytes 1572868
  115.0 33.9 %copy-start.2 = (bf16[512,256]{1,0:T(8,128)(2,1)S(1)}, bf16[512,256]{1,0:T(8,128)(2,1)}, u32[]{:S(2)}) copy-start(bf16[512,256]{1,0:T(8,128)(2,1)} %ffn_out.1) | copy-start | bytes 786436
  115.0 33.9 %copy-start.3 = (bf16[256,256]{1,0:T(8,128)(2,1)S(1)}, bf16[256,256]{1,0:T(8,128)(2,1)}, u32[]{:S(2)}) copy-start(bf16[256,256]{1,0:T(8,128)(2,1)} %out_proj.1) | copy-start | bytes 393220
  115.0 33.9 %copy-start.5 = (f32[512]{0:T(512)S(1)}, f32[512]{0:T(512)}, u32[]{:S(2)}) copy-start(f32[512]{0:T(512)} %param.20) | copy-start | bytes 6148
  115.0 33.9 %copy-start.6 = (f32[512]{0:T(512)S(1)}, f32[512]{0:T(512)}, u32[]{:S(2)}) copy-start(f32[512]{0:T(512)} %param.21) | copy-start | bytes 6148
  138.0 11.0 %copy-start = (f32[4,256,256]{2,1,0:T(8,128)S(1)}, f32[4,256,256]{2,1,0:T(8,128)}, u32[]{:S(2)}) copy-start(f32[4,256,256]{2,1,0:T(8,128)} %features.1) | copy-start | bytes 3145732
  138.0 10.9 %all-to-all-start.3 = ((bf16[4,512,128]{2,1,0:T(8,128)(2,1)}), bf16[4,512,128]{2,1,0:T(8,128)(2,1)S(1)}, u32[]{:S(2)}, u32[]{:S(2)}) async-start(bf16[4,512,128]{2,1,0:T(8,128)(2,1)} %attend_2.1), calls=%async_computation.3 | async-start | bytes 1048576 | tf_op jit(solution)/shard_map/all_to_all | solution.py:34
  148.9 0.7 copy-start.4
  148.9 0.7 copy-start.7
